TPU v7x, 512 devices: a whole 4x8x8 slice. The times are simulated.
512 devices in a mesh: layer: 8 (over z), row: 8 (over x, core), col: 8 (over y).
Axes of the slice: x: 4, y: 8, z: 8, core: 2. Of those that a mesh axis runs over, the one named last changes fastest.
Arguments:
- c_states: float32 [8, 64, 64, 1024], P('layer', None, 'row', 'col'), may hold values from -6 to 6
- c_adjoints: float32 [8, 64, 64, 1024], P('layer', None, 'row', 'col'), may hold values from -6 to 6
- weights: bfloat16 [32, 64, 576], P('layer'), may hold values from -0.25 to 0.25
Outputs:
- new_states: float32 [8, 64, 64, 1024], P('layer', None, 'row', 'col')
- new_adjoints: float32 [8, 64, 64, 1024], P('layer', None, 'row', 'col')
- weight_grads: float32 [32, 64, 576], P('layer')
All inputs are finite; a program needn't handle non-finite values.
Results may differ from a plain program's by a relative error of at most 0.006.
Values may be sent and summed in bfloat16 or wider, within the bound.
A program may use at most 64 MiB of HBM per device.

v0:
```python
import jax
import jax.numpy as jnp
from jax import lax
from jax.sharding import PartitionSpec as P

step_size = 0.2


def with_halo(cells, sides, width):
    for axis, dim in sides:
        count = lax.axis_size(axis)
        ends = count - 1
        head = lax.slice_in_dim(cells, 0, width, axis=dim)
        tail = lax.slice_in_dim(cells, cells.shape[dim] - width, cells.shape[dim], axis=dim)
        cells = jnp.concatenate(
            [
                lax.ppermute(tail, axis, [(i, (i + 1) % count) for i in range(ends)]),
                cells,
                lax.ppermute(head, axis, [((i + 1) % count, i) for i in range(ends)]),
            ],
            axis=dim,
        )
    return cells


def from_behind(array, axis, by):
    devices = lax.axis_size(axis)
    pairs = [(i, i + by) for i in range(devices) if 0 <= i + by < devices]
    return lax.ppermute(array, axis, pairs)


def tile_patches(padded, tile_rows, tile_cols):
    shifted = [
        padded[:, row_off : row_off + tile_rows, col_off : col_off + tile_cols].reshape(
            padded.shape[0], tile_rows * tile_cols
        )
        for row_off in range(3)
        for col_off in range(3)
    ]
    return jnp.concatenate(shifted, 0)


def exact_dot(left_mat, right_mat):
    return jnp.dot(
        left_mat, right_mat, precision=lax.Precision.HIGHEST, preferred_element_type=jnp.float32
    )


def flipped(weight_mat):
    channels = weight_mat.shape[0]
    return jnp.transpose(weight_mat.reshape(channels, 9, channels)[:, ::-1, :], (2, 1, 0)).reshape(
        channels, 9 * channels
    )


def local(c_states, c_adjoints, weights):
    group_index = lax.axis_index("layer")
    group_count = lax.axis_size("layer")
    channels, tile_rows, tile_cols = c_states.shape[1:]
    pixels = tile_rows * tile_cols
    depth = weights.shape[0]
    initial_flat = c_states[0].reshape(channels, pixels)
    guess_flat = c_adjoints[0].reshape(channels, pixels)

    def advance(state, weight_mat):
        active = state.astype(jnp.bfloat16).reshape(channels, tile_rows, tile_cols)
        padded = with_halo(active, (("row", 1), ("col", 2)), 1)
        preact = jnp.dot(
            weight_mat,
            tile_patches(padded, tile_rows, tile_cols),
            preferred_element_type=jnp.float32,
        )
        return (state + step_size * jnp.tanh(preact), padded, preact)

    state = initial_flat
    for layer_pos in range(depth):
        state, _, _ = advance(state, weights[layer_pos])
    group_end = state
    summed = jnp.sum(weights[0].astype(jnp.float32).reshape(channels, 9, channels), axis=1)
    coarse_map = jnp.eye(channels, dtype=jnp.float32) + step_size * summed
    is_first = group_index == 0
    is_last = group_index == group_count - 1
    zero_map = jnp.zeros_like(coarse_map)
    blank = jnp.zeros((channels, pixels), jnp.float32)
    fwd_map = jnp.where(is_first, zero_map, coarse_map)
    fwd_offset = jnp.where(is_first, group_end, group_end - exact_dot(coarse_map, initial_flat))

    def state_turn(turn_number, carried):
        return from_behind(exact_dot(fwd_map, carried) + fwd_offset, "layer", 1)

    arrived = lax.fori_loop(0, group_count - 1, state_turn, blank)
    corrected = jnp.where(is_first, initial_flat, arrived)
    state = corrected
    trail = []
    for layer_pos in range(depth):
        state, padded, preact = advance(state, weights[layer_pos])
        trail.append((padded, preact))
    adjoint = guess_flat
    grad_list = [None] * depth
    for layer_pos in reversed(range(depth)):
        padded, preact = trail[layer_pos]
        slope = jnp.tanh(preact)
        source = (adjoint * step_size * (1.0 - slope * slope)).astype(jnp.bfloat16)
        source_pad = with_halo(
            source.reshape(channels, tile_rows, tile_cols), (("row", 1), ("col", 2)), 1
        )
        grad_list[layer_pos] = lax.dot_general(
            source,
            tile_patches(padded, tile_rows, tile_cols),
            (((1,), (1,)), ((), ())),
            preferred_element_type=jnp.float32,
        )
        back = jnp.dot(
            flipped(weights[layer_pos]),
            tile_patches(source_pad, tile_rows, tile_cols),
            preferred_element_type=jnp.float32,
        )
        adjoint = adjoint + back
    weight_grads = lax.psum(jnp.stack(grad_list, 0), ("row", "col"))
    transposed = coarse_map.T
    back_map = jnp.where(is_last, zero_map, transposed)
    back_offset = jnp.where(is_last, adjoint, adjoint - exact_dot(transposed, guess_flat))

    def adjoint_turn(turn_number, carried):
        return from_behind(exact_dot(back_map, carried) + back_offset, "layer", -1)

    returned = lax.fori_loop(0, group_count - 1, adjoint_turn, blank)
    new_adjoint = jnp.where(is_last, guess_flat, returned)
    out_shape = (1, channels, tile_rows, tile_cols)
    return (corrected.reshape(out_shape), new_adjoint.reshape(out_shape), weight_grads)


def solution(mesh):
    placed = (
        P("layer", None, "row", "col"),
        P("layer", None, "row", "col"),
        P("layer", None, None),
    )
    return jax.shard_map(
        local,
        mesh=mesh,
        in_specs=placed,
        out_specs=(
            P("layer", None, "row", "col"),
            P("layer", None, "row", "col"),
            P("layer", None, None),
        ),
        check_vma=False,
    )
```

profile of v0, /device:TPU:1, one launch (start us, length us, event | category | flops | bytes accessed | tf_op | source)
XLA Modules:
  0.0 560.1 jit_solution(8448254401400745606)
XLA Ops:
  8.2 4.5 collective-permute-start.2
  12.8 5.6 collective-permute-start.3
  22.8 4.6 collective-permute-done.4
  27.9 3.7 collective-permute-done.5
  38.6 3.3 collective-permute-done.7
  50.3 3.6 collective-permute-done.9
  55.3 3.9 collective-permute-start.10
  64.7 5.2 collective-permute-start.12
  74.9 4.8 collective-permute-done.13
  81.0 4.5 collective-permute-start.14
  91.1 3.8 collective-permute-start.16
  99.8 3.7 collective-permute-done.17
  105.2 64.2 %while.20 = (s32[]{:T(128)}, f32[64,1024]{1,0:T(8,128)S(1)}, f32[64,64]{1,0:T(8,128)S(1)}, f32[64,1024]{1,0:T(8,128)S(1)}, s32[]{:T(128)}) while((s32[]{:T(128)}, f32[64,1024]{1,0:T(8,128)S(1)}, f32[64,64]{1,0:T(8,128)S(1)}, f32[64,1024]{1,0:T(8,128)S(1)}, s32[]{:T(128)}) %tuple.143), condition=%wide.region_2.3_spmd, body=%wide.region_1.2_spmd.sunk | while | flops 50397184 | bytes 1851493 | solution.py:91
  105.6 4.0 collective-permute-start
  109.6 5.8 %collective-permute-done = f32[64,1024]{1,0:T(8,128)S(1)} collective-permute-done((f32[64,1024]{1,0:T(8,128)S(1)}, f32[64,1024]{1,0:T(8,128)S(1)}, u32[]{:S(2)}, u32[]{:S(2)}) %collective-permute-start) | collective-permute-done | bytes 262176 | tf_op jit(solution)/shard_map/while/body/eval_jaxpr/ppermute | solution.py:29
  115.8 4.0 collective-permute-start
  119.8 5.5 collective-permute-done
  125.7 4.1 collective-permute-start
  129.8 4.5 collective-permute-done
  134.7 5.4 collective-permute-start
  140.1 3.8 collective-permute-done
  144.3 4.1 collective-permute-start
  152.0 5.1 collective-permute-start
  160.8 5.3 collective-permute-start
  169.5 6.1 %collective-permute-start.18 = (bf16[64,1,128]{2,1,0:T(2,128)(2,1)S(1)}, bf16[64,1,128]{2,1,0:T(2,128)(2,1)S(1)}, u32[]{:S(2)}, u32[]{:S(2)}) collective-permute-start(bf16[64,1,128]{2,1,0:T(2,128)(2,1)S(1)} %get-tuple-element.215), channel_id=1, source_target_pairs={{0,8},{8,16},{16,24},{24,32},{32,40},{40,48},{48,56},{1,9},{9,17},... | collective-permute-start | bytes 49160 | tf_op jit(solution)/shard_map/ppermute | solution.py:17
  185.0 3.7 collective-permute-done.20
  189.2 3.6 collective-permute-done.21
  202.2 3.9 collective-permute-start.24
  211.0 4.6 collective-permute-done.25
  217.8 4.2 collective-permute-start.26
  228.2 3.5 collective-permute-start.28
  251.3 3.7 collective-permute-start.32
  260.7 3.8 collective-permute-done.33
  277.7 3.4 collective-permute-start.36
  288.2 6.2 %collective-permute-done.37 = bf16[64,10,1]{2,1,0:T(8,128)(2,1)S(1)} collective-permute-done((bf16[64,10,1]{2,1,0:T(8,128)(2,1)}, bf16[64,10,1]{2,1,0:T(8,128)(2,1)S(1)}, u32[]{:S(2)}, u32[]{:S(2)}) %collective-permute-start.37) | collective-permute-done | bytes 1312 | tf_op jit(solution)/shard_map/ppermute | solution.py:19
  313.3 4.2 collective-permute-done.40
  318.0 4.1 collective-permute-done.41
  340.3 4.1 collective-permute-done.45
  362.3 4.5 collective-permute-done.49
  369.2 71.1 %while.21 = (s32[]{:T(128)}, f32[64,1024]{1,0:T(8,128)S(1)}, f32[64,64]{1,0:T(8,128)S(1)}, f32[64,1024]{1,0:T(8,128)S(1)}, s32[]{:T(128)}) while((s32[]{:T(128)}, f32[64,1024]{1,0:T(8,128)S(1)}, f32[64,64]{1,0:T(8,128)S(1)}, f32[64,1024]{1,0:T(8,128)S(1)}, s32[]{:T(128)}) %tuple.146), condition=%wide.region_4.5_spmd, body=%wide.region_3.4_spmd.sunk | while | flops 50397184 | bytes 1851493 | solution.py:127
  370.9 10.6 %collective-permute-done.1 = f32[64,1024]{1,0:T(8,128)S(1)} collective-permute-done((f32[64,1024]{1,0:T(8,128)S(1)}, f32[64,1024]{1,0:T(8,128)S(1)}, u32[]{:S(2)}, u32[]{:S(2)}) %collective-permute-start.1) | collective-permute-done | bytes 262176 | tf_op jit(solution)/shard_map/while/body/eval_jaxpr/ppermute | solution.py:29
  383.2 10.7 %collective-permute-done.1 = f32[64,1024]{1,0:T(8,128)S(1)} collective-permute-done((f32[64,1024]{1,0:T(8,128)S(1)}, f32[64,1024]{1,0:T(8,128)S(1)}, u32[]{:S(2)}, u32[]{:S(2)}) %collective-permute-start.1) | collective-permute-done | bytes 262176 | tf_op jit(solution)/shard_map/while/body/eval_jaxpr/ppermute | solution.py:29
  395.6 10.1 %collective-permute-done.1 = f32[64,1024]{1,0:T(8,128)S(1)} collective-permute-done((f32[64,1024]{1,0:T(8,128)S(1)}, f32[64,1024]{1,0:T(8,128)S(1)}, u32[]{:S(2)}, u32[]{:S(2)}) %collective-permute-start.1) | collective-permute-done | bytes 262176 | tf_op jit(solution)/shard_map/while/body/eval_jaxpr/ppermute | solution.py:29
  407.3 9.0 %collective-permute-done.1 = f32[64,1024]{1,0:T(8,128)S(1)} collective-permute-done((f32[64,1024]{1,0:T(8,128)S(1)}, f32[64,1024]{1,0:T(8,128)S(1)}, u32[]{:S(2)}, u32[]{:S(2)}) %collective-permute-start.1) | collective-permute-done | bytes 262176 | tf_op jit(solution)/shard_map/while/body/eval_jaxpr/ppermute | solution.py:29
  418.0 6.4 %collective-permute-done.1 = f32[64,1024]{1,0:T(8,128)S(1)} collective-permute-done((f32[64,1024]{1,0:T(8,128)S(1)}, f32[64,1024]{1,0:T(8,128)S(1)}, u32[]{:S(2)}, u32[]{:S(2)}) %collective-permute-start.1) | collective-permute-done | bytes 262176 | tf_op jit(solution)/shard_map/while/body/eval_jaxpr/ppermute | solution.py:29
  426.1 5.8 %collective-permute-done.1 = f32[64,1024]{1,0:T(8,128)S(1)} collective-permute-done((f32[64,1024]{1,0:T(8,128)S(1)}, f32[64,1024]{1,0:T(8,128)S(1)}, u32[]{:S(2)}, u32[]{:S(2)}) %collective-permute-start.1) | collective-permute-done | bytes 262176 | tf_op jit(solution)/shard_map/while/body/eval_jaxpr/ppermute | solution.py:29
  433.5 6.8 %collective-permute-done.1 = f32[64,1024]{1,0:T(8,128)S(1)} collective-permute-done((f32[64,1024]{1,0:T(8,128)S(1)}, f32[64,1024]{1,0:T(8,128)S(1)}, u32[]{:S(2)}, u32[]{:S(2)}) %collective-permute-start.1) | collective-permute-done | bytes 262176 | tf_op jit(solution)/shard_map/while/body/eval_jaxpr/ppermute | solution.py:29
  441.1 110.2 %all-reduce.2.cloned.1.call-done = f32[4,64,576]{2,1,0:T(8,128)} async-done(((f32[4,64,576]{2,1,0:T(8,128)}), f32[4,64,576]{2,1,0:T(8,128)}) %all-reduce.2.cloned.1.call-update) | async-done | bytes 589840 | tf_op jit(solution)/shard_map/psum | solution.py:119
  (376 shorter events, 207.8 us)
Async XLA Ops:
  7.2 544.2 %all-reduce.2.cloned.1.call-start = ((), (), s32[]{:S(2)}) async-start(), calls=%async_computation | async-start | bytes 1310720 | tf_op jit(solution)/shard_map/psum | solution.py:119
  8.2 10.1 %collective-permute-start.2 = (bf16[64,1,128]{2,1,0:T(2,128)(2,1)S(1)}, bf16[64,1,128]{2,1,0:T(2,128)(2,1)S(1)}, u32[]{:S(2)}, u32[]{:S(2)}) collective-permute-start(bf16[64,1,128]{2,1,0:T(2,128)(2,1)S(1)} %get-tuple-element.223), channel_id=1, source_target_pairs={{0,8},{8,16},{16,24},{24,32},{32,40},{40,48},{48,56},{1,9},{9,17},... | collective-permute-start | bytes 49160 | tf_op jit(solution)/shard_map/ppermute | solution.py:17
  12.8 6.4 %collective-permute-start.3 = (bf16[64,1,128]{2,1,0:T(2,128)(2,1)S(1)}, bf16[64,1,128]{2,1,0:T(2,128)(2,1)S(1)}, u32[]{:S(2)}, u32[]{:S(2)}) collective-permute-start(bf16[64,1,128]{2,1,0:T(2,128)(2,1)S(1)} %get-tuple-element.224), channel_id=1, source_target_pairs={{8,0},{16,8},{24,16},{32,24},{40,32},{48,40},{56,48},{9,1},{17,9},... | collective-permute-start | bytes 49160 | tf_op jit(solution)/shard_map/ppermute | solution.py:19
  19.5 7.9 %collective-permute-start.4 = (bf16[64,10,1]{2,1,0:T(8,128)(2,1)S(1)}, bf16[64,10,1]{2,1,0:T(8,128)(2,1)S(1)}, u32[]{:S(2)}, u32[]{:S(2)}) collective-permute-start(bf16[64,10,1]{2,1,0:T(8,128)(2,1)S(1)} %get-tuple-element.176), channel_id=1, source_target_pairs={{0,1},{1,2},{2,3},{3,4},{4,5},{5,6},{6,7},{8,9},{9,10},{10,11},{11... | collective-permute-start | bytes 3848 | tf_op jit(solution)/shard_map/ppermute | solution.py:17
  21.5 10.1 %collective-permute-start.5 = (bf16[64,10,1]{2,1,0:T(8,128)(2,1)S(1)}, bf16[64,10,1]{2,1,0:T(8,128)(2,1)S(1)}, u32[]{:S(2)}, u32[]{:S(2)}) collective-permute-start(bf16[64,10,1]{2,1,0:T(8,128)(2,1)S(1)} %get-tuple-element.175), channel_id=1, source_target_pairs={{1,0},{2,1},{3,2},{4,3},{5,4},{6,5},{7,6},{9,8},{10,9},{11,10},{12... | collective-permute-start | bytes 3848 | tf_op jit(solution)/shard_map/ppermute | solution.py:19
  42.2 7.6 %collective-permute-start.8 = (bf16[64,10,1]{2,1,0:T(8,128)(2,1)S(1)}, bf16[64,10,1]{2,1,0:T(8,128)(2,1)S(1)}, u32[]{:S(2)}, u32[]{:S(2)}) collective-permute-start(bf16[64,10,1]{2,1,0:T(8,128)(2,1)S(1)} %get-tuple-element.174), channel_id=1, source_target_pairs={{0,1},{1,2},{2,3},{3,4},{4,5},{5,6},{6,7},{8,9},{9,10},{10,11},{11... | collective-permute-start | bytes 3848 | tf_op jit(solution)/shard_map/ppermute | solution.py:17
  45.4 8.5 %collective-permute-start.9 = (bf16[64,10,1]{2,1,0:T(8,128)(2,1)S(1)}, bf16[64,10,1]{2,1,0:T(8,128)(2,1)S(1)}, u32[]{:S(2)}, u32[]{:S(2)}) collective-permute-start(bf16[64,10,1]{2,1,0:T(8,128)(2,1)S(1)} %get-tuple-element.173), channel_id=1, source_target_pairs={{1,0},{2,1},{3,2},{4,3},{5,4},{6,5},{7,6},{9,8},{10,9},{11,10},{12... | collective-permute-start | bytes 3848 | tf_op jit(solution)/shard_map/ppermute | solution.py:19
  55.3 5.8 %collective-permute-start.10 = (bf16[64,1,128]{2,1,0:T(2,128)(2,1)S(1)}, bf16[64,1,128]{2,1,0:T(2,128)(2,1)S(1)}, u32[]{:S(2)}, u32[]{:S(2)}) collective-permute-start(bf16[64,1,128]{2,1,0:T(2,128)(2,1)S(1)} %get-tuple-element.219), channel_id=1, source_target_pairs={{0,8},{8,16},{16,24},{24,32},{32,40},{40,48},{48,56},{1,9},{9,17},... | collective-permute-start | bytes 49160 | tf_op jit(solution)/shard_map/ppermute | solution.py:17
  64.7 9.7 %collective-permute-start.12 = (bf16[64,10,1]{2,1,0:T(8,128)(2,1)S(1)}, bf16[64,10,1]{2,1,0:T(8,128)(2,1)S(1)}, u32[]{:S(2)}, u32[]{:S(2)}) collective-permute-start(bf16[64,10,1]{2,1,0:T(8,128)(2,1)S(1)} %get-tuple-element.172), channel_id=1, source_target_pairs={{0,1},{1,2},{2,3},{3,4},{4,5},{5,6},{6,7},{8,9},{9,10},{10,11},{11... | collective-permute-start | bytes 3848 | tf_op jit(solution)/shard_map/ppermute | solution.py:17
  70.8 8.9 %collective-permute-start.13 = (bf16[64,10,1]{2,1,0:T(8,128)(2,1)S(1)}, bf16[64,10,1]{2,1,0:T(8,128)(2,1)S(1)}, u32[]{:S(2)}, u32[]{:S(2)}) collective-permute-start(bf16[64,10,1]{2,1,0:T(8,128)(2,1)S(1)} %get-tuple-element.171), channel_id=1, source_target_pairs={{1,0},{2,1},{3,2},{4,3},{5,4},{6,5},{7,6},{9,8},{10,9},{11,10},{12... | collective-permute-start | bytes 3848 | tf_op jit(solution)/shard_map/ppermute | solution.py:19
  81.0 6.5 %collective-permute-start.14 = (bf16[64,1,128]{2,1,0:T(2,128)(2,1)S(1)}, bf16[64,1,128]{2,1,0:T(2,128)(2,1)S(1)}, u32[]{:S(2)}, u32[]{:S(2)}) collective-permute-start(bf16[64,1,128]{2,1,0:T(2,128)(2,1)S(1)} %get-tuple-element.217), channel_id=1, source_target_pairs={{0,8},{8,16},{16,24},{24,32},{32,40},{40,48},{48,56},{1,9},{9,17},... | collective-permute-start | bytes 49160 | tf_op jit(solution)/shard_map/ppermute | solution.py:17
  91.1 8.2 %collective-permute-start.16 = (bf16[64,10,1]{2,1,0:T(8,128)(2,1)S(1)}, bf16[64,10,1]{2,1,0:T(8,128)(2,1)S(1)}, u32[]{:S(2)}, u32[]{:S(2)}) collective-permute-start(bf16[64,10,1]{2,1,0:T(8,128)(2,1)S(1)} %get-tuple-element.170), channel_id=1, source_target_pairs={{0,1},{1,2},{2,3},{3,4},{4,5},{5,6},{6,7},{8,9},{9,10},{10,11},{11... | collective-permute-start | bytes 3848 | tf_op jit(solution)/shard_map/ppermute | solution.py:17
  95.0 8.5 %collective-permute-start.17 = (bf16[64,10,1]{2,1,0:T(8,128)(2,1)S(1)}, bf16[64,10,1]{2,1,0:T(8,128)(2,1)S(1)}, u32[]{:S(2)}, u32[]{:S(2)}) collective-permute-start(bf16[64,10,1]{2,1,0:T(8,128)(2,1)S(1)} %get-tuple-element.169), channel_id=1, source_target_pairs={{1,0},{2,1},{3,2},{4,3},{5,4},{6,5},{7,6},{9,8},{10,9},{11,10},{12... | collective-permute-start | bytes 3848 | tf_op jit(solution)/shard_map/ppermute | solution.py:19
  105.6 9.8 %collective-permute-start = (f32[64,1024]{1,0:T(8,128)S(1)}, f32[64,1024]{1,0:T(8,128)S(1)}, u32[]{:S(2)}, u32[]{:S(2)}) collective-permute-start(f32[64,1024]{1,0:T(8,128)S(1)} %convolution_add_fusion.4), channel_id=1, source_target_pairs={{0,64},{64,128},{128,192},{192,256},{256,320},{320,384},{384,448},... | collective-permute-start | bytes 786440 | tf_op jit(solution)/shard_map/while/body/eval_jaxpr/ppermute | solution.py:29
  115.8 9.5 %collective-permute-start = (f32[64,1024]{1,0:T(8,128)S(1)}, f32[64,1024]{1,0:T(8,128)S(1)}, u32[]{:S(2)}, u32[]{:S(2)}) collective-permute-start(f32[64,1024]{1,0:T(8,128)S(1)} %convolution_add_fusion.4), channel_id=1, source_target_pairs={{0,64},{64,128},{128,192},{192,256},{256,320},{320,384},{384,448},... | collective-permute-start | bytes 786440 | tf_op jit(solution)/shard_map/while/body/eval_jaxpr/ppermute | solution.py:29
  125.7 8.7 %collective-permute-start = (f32[64,1024]{1,0:T(8,128)S(1)}, f32[64,1024]{1,0:T(8,128)S(1)}, u32[]{:S(2)}, u32[]{:S(2)}) collective-permute-start(f32[64,1024]{1,0:T(8,128)S(1)} %convolution_add_fusion.4), channel_id=1, source_target_pairs={{0,64},{64,128},{128,192},{192,256},{256,320},{320,384},{384,448},... | collective-permute-start | bytes 786440 | tf_op jit(solution)/shard_map/while/body/eval_jaxpr/ppermute | solution.py:29
  134.7 9.2 %collective-permute-start = (f32[64,1024]{1,0:T(8,128)S(1)}, f32[64,1024]{1,0:T(8,128)S(1)}, u32[]{:S(2)}, u32[]{:S(2)}) collective-permute-start(f32[64,1024]{1,0:T(8,128)S(1)} %convolution_add_fusion.4), channel_id=1, source_target_pairs={{0,64},{64,128},{128,192},{192,256},{256,320},{320,384},{384,448},... | collective-permute-start | bytes 786440 | tf_op jit(solution)/shard_map/while/body/eval_jaxpr/ppermute | solution.py:29
  144.3 7.4 %collective-permute-start = (f32[64,1024]{1,0:T(8,128)S(1)}, f32[64,1024]{1,0:T(8,128)S(1)}, u32[]{:S(2)}, u32[]{:S(2)}) collective-permute-start(f32[64,1024]{1,0:T(8,128)S(1)} %convolution_add_fusion.4), channel_id=1, source_target_pairs={{0,64},{64,128},{128,192},{192,256},{256,320},{320,384},{384,448},... | collective-permute-start | bytes 786440 | tf_op jit(solution)/shard_map/while/body/eval_jaxpr/ppermute | solution.py:29
  152.0 8.3 %collective-permute-start = (f32[64,1024]{1,0:T(8,128)S(1)}, f32[64,1024]{1,0:T(8,128)S(1)}, u32[]{:S(2)}, u32[]{:S(2)}) collective-permute-start(f32[64,1024]{1,0:T(8,128)S(1)} %convolution_add_fusion.4), channel_id=1, source_target_pairs={{0,64},{64,128},{128,192},{192,256},{256,320},{320,384},{384,448},... | collective-permute-start | bytes 786440 | tf_op jit(solution)/shard_map/while/body/eval_jaxpr/ppermute | solution.py:29
  160.8 8.6 %collective-permute-start = (f32[64,1024]{1,0:T(8,128)S(1)}, f32[64,1024]{1,0:T(8,128)S(1)}, u32[]{:S(2)}, u32[]{:S(2)}) collective-permute-start(f32[64,1024]{1,0:T(8,128)S(1)} %convolution_add_fusion.4), channel_id=1, source_target_pairs={{0,64},{64,128},{128,192},{192,256},{256,320},{320,384},{384,448},... | collective-permute-start | bytes 786440 | tf_op jit(solution)/shard_map/while/body/eval_jaxpr/ppermute | solution.py:29
  169.5 9.0 %collective-permute-start.18 = (bf16[64,1,128]{2,1,0:T(2,128)(2,1)S(1)}, bf16[64,1,128]{2,1,0:T(2,128)(2,1)S(1)}, u32[]{:S(2)}, u32[]{:S(2)}) collective-permute-start(bf16[64,1,128]{2,1,0:T(2,128)(2,1)S(1)} %get-tuple-element.215), channel_id=1, source_target_pairs={{0,8},{8,16},{16,24},{24,32},{32,40},{40,48},{48,56},{1,9},{9,17},... | collective-permute-start | bytes 49160 | tf_op jit(solution)/shard_map/ppermute | solution.py:17
  181.1 7.6 %collective-permute-start.20 = (bf16[64,10,1]{2,1,0:T(8,128)(2,1)S(1)}, bf16[64,10,1]{2,1,0:T(8,128)(2,1)S(1)}, u32[]{:S(2)}, u32[]{:S(2)}) collective-permute-start(bf16[64,10,1]{2,1,0:T(8,128)(2,1)S(1)} %get-tuple-element.168), channel_id=1, source_target_pairs={{0,1},{1,2},{2,3},{3,4},{4,5},{5,6},{6,7},{8,9},{9,10},{10,11},{11... | collective-permute-start | bytes 3848 | tf_op jit(solution)/shard_map/ppermute | solution.py:17
  183.5 9.3 %collective-permute-start.21 = (bf16[64,10,1]{2,1,0:T(8,128)(2,1)S(1)}, bf16[64,10,1]{2,1,0:T(8,128)(2,1)S(1)}, u32[]{:S(2)}, u32[]{:S(2)}) collective-permute-start(bf16[64,10,1]{2,1,0:T(8,128)(2,1)S(1)} %get-tuple-element.167), channel_id=1, source_target_pairs={{1,0},{2,1},{3,2},{4,3},{5,4},{6,5},{7,6},{9,8},{10,9},{11,10},{12... | collective-permute-start | bytes 3848 | tf_op jit(solution)/shard_map/ppermute | solution.py:19
  202.2 8.3 %collective-permute-start.24 = (bf16[64,10,1]{2,1,0:T(8,128)(2,1)S(1)}, bf16[64,10,1]{2,1,0:T(8,128)(2,1)S(1)}, u32[]{:S(2)}, u32[]{:S(2)}) collective-permute-start(bf16[64,10,1]{2,1,0:T(8,128)(2,1)S(1)} %get-tuple-element.166), channel_id=1, source_target_pairs={{0,1},{1,2},{2,3},{3,4},{4,5},{5,6},{6,7},{8,9},{9,10},{10,11},{11... | collective-permute-start | bytes 3848 | tf_op jit(solution)/shard_map/ppermute | solution.py:17
  206.1 9.6 %collective-permute-start.25 = (bf16[64,10,1]{2,1,0:T(8,128)(2,1)S(1)}, bf16[64,10,1]{2,1,0:T(8,128)(2,1)S(1)}, u32[]{:S(2)}, u32[]{:S(2)}) collective-permute-start(bf16[64,10,1]{2,1,0:T(8,128)(2,1)S(1)} %get-tuple-element.165), channel_id=1, source_target_pairs={{1,0},{2,1},{3,2},{4,3},{5,4},{6,5},{7,6},{9,8},{10,9},{11,10},{12... | collective-permute-start | bytes 3848 | tf_op jit(solution)/shard_map/ppermute | solution.py:19
  217.8 6.1 %collective-permute-start.26 = (bf16[64,1,128]{2,1,0:T(2,128)(2,1)S(1)}, bf16[64,1,128]{2,1,0:T(2,128)(2,1)S(1)}, u32[]{:S(2)}, u32[]{:S(2)}) collective-permute-start(bf16[64,1,128]{2,1,0:T(2,128)(2,1)S(1)} %get-tuple-element.211), channel_id=1, source_target_pairs={{0,8},{8,16},{16,24},{24,32},{32,40},{40,48},{48,56},{1,9},{9,17},... | collective-permute-start | bytes 49160 | tf_op jit(solution)/shard_map/ppermute | solution.py:17
  228.2 7.6 %collective-permute-start.28 = (bf16[64,10,1]{2,1,0:T(8,128)(2,1)}, bf16[64,10,1]{2,1,0:T(8,128)(2,1)}, u32[]{:S(2)}, u32[]{:S(2)}) collective-permute-start(bf16[64,10,1]{2,1,0:T(8,128)(2,1)} %get-tuple-element.164), channel_id=1, source_target_pairs={{0,1},{1,2},{2,3},{3,4},{4,5},{5,6},{6,7},{8,9},{9,10},{10,11},{11... | collective-permute-start | bytes 3848 | tf_op jit(solution)/shard_map/ppermute | solution.py:17
  231.7 8.7 %collective-permute-start.29 = (bf16[64,10,1]{2,1,0:T(8,128)(2,1)}, bf16[64,10,1]{2,1,0:T(8,128)(2,1)S(1)}, u32[]{:S(2)}, u32[]{:S(2)}) collective-permute-start(bf16[64,10,1]{2,1,0:T(8,128)(2,1)} %get-tuple-element.163), channel_id=1, source_target_pairs={{1,0},{2,1},{3,2},{4,3},{5,4},{6,5},{7,6},{9,8},{10,9},{11,10},{12... | collective-permute-start | bytes 3848 | tf_op jit(solution)/shard_map/ppermute | solution.py:19
  251.3 7.7 %collective-permute-start.32 = (bf16[64,10,1]{2,1,0:T(8,128)(2,1)}, bf16[64,10,1]{2,1,0:T(8,128)(2,1)}, u32[]{:S(2)}, u32[]{:S(2)}) collective-permute-start(bf16[64,10,1]{2,1,0:T(8,128)(2,1)} %get-tuple-element.162), channel_id=1, source_target_pairs={{0,1},{1,2},{2,3},{3,4},{4,5},{5,6},{6,7},{8,9},{9,10},{10,11},{11... | collective-permute-start | bytes 3848 | tf_op jit(solution)/shard_map/ppermute | solution.py:17
  255.7 8.7 %collective-permute-start.33 = (bf16[64,10,1]{2,1,0:T(8,128)(2,1)}, bf16[64,10,1]{2,1,0:T(8,128)(2,1)S(1)}, u32[]{:S(2)}, u32[]{:S(2)}) collective-permute-start(bf16[64,10,1]{2,1,0:T(8,128)(2,1)} %get-tuple-element.161), channel_id=1, source_target_pairs={{1,0},{2,1},{3,2},{4,3},{5,4},{6,5},{7,6},{9,8},{10,9},{11,10},{12... | collective-permute-start | bytes 3848 | tf_op jit(solution)/shard_map/ppermute | solution.py:19
  268.5 6.0 %collective-permute-start.34 = (bf16[64,1,128]{2,1,0:T(2,128)(2,1)}, bf16[64,1,128]{2,1,0:T(2,128)(2,1)S(1)}, u32[]{:S(2)}, u32[]{:S(2)}) collective-permute-start(bf16[64,1,128]{2,1,0:T(2,128)(2,1)} %get-tuple-element.207), channel_id=1, source_target_pairs={{0,8},{8,16},{16,24},{24,32},{32,40},{40,48},{48,56},{1,9},{9,17},... | collective-permute-start | bytes 49160 | tf_op jit(solution)/shard_map/ppermute | solution.py:17
  277.7 8.7 %collective-permute-start.36 = (bf16[64,10,1]{2,1,0:T(8,128)(2,1)}, bf16[64,10,1]{2,1,0:T(8,128)(2,1)}, u32[]{:S(2)}, u32[]{:S(2)}) collective-permute-start(bf16[64,10,1]{2,1,0:T(8,128)(2,1)} %get-tuple-element.160), channel_id=1, source_target_pairs={{0,1},{1,2},{2,3},{3,4},{4,5},{5,6},{6,7},{8,9},{9,10},{10,11},{11... | collective-permute-start | bytes 3848 | tf_op jit(solution)/shard_map/ppermute | solution.py:17
  285.2 9.3 %collective-permute-start.37 = (bf16[64,10,1]{2,1,0:T(8,128)(2,1)}, bf16[64,10,1]{2,1,0:T(8,128)(2,1)S(1)}, u32[]{:S(2)}, u32[]{:S(2)}) collective-permute-start(bf16[64,10,1]{2,1,0:T(8,128)(2,1)} %get-tuple-element.159), channel_id=1, source_target_pairs={{1,0},{2,1},{3,2},{4,3},{5,4},{6,5},{7,6},{9,8},{10,9},{11,10},{12... | collective-permute-start | bytes 3848 | tf_op jit(solution)/shard_map/ppermute | solution.py:19
  298.8 9.9 %collective-permute-start.38 = (bf16[64,1,128]{2,1,0:T(2,128)(2,1)}, bf16[64,1,128]{2,1,0:T(2,128)(2,1)S(1)}, u32[]{:S(2)}, u32[]{:S(2)}) collective-permute-start(bf16[64,1,128]{2,1,0:T(2,128)(2,1)} %get-tuple-element.205), channel_id=1, source_target_pairs={{0,8},{8,16},{16,24},{24,32},{32,40},{40,48},{48,56},{1,9},{9,17},... | collective-permute-start | bytes 49160 | tf_op jit(solution)/shard_map/ppermute | solution.py:17
  300.7 8.0 %collective-permute-start.39 = (bf16[64,1,128]{2,1,0:T(2,128)(2,1)}, bf16[64,1,128]{2,1,0:T(2,128)(2,1)S(1)}, u32[]{:S(2)}, u32[]{:S(2)}) collective-permute-start(bf16[64,1,128]{2,1,0:T(2,128)(2,1)} %get-tuple-element.206), channel_id=1, source_target_pairs={{8,0},{16,8},{24,16},{32,24},{40,32},{48,40},{56,48},{9,1},{17,9},... | collective-permute-start | bytes 49160 | tf_op jit(solution)/shard_map/ppermute | solution.py:19
  309.0 8.4 %collective-permute-start.40 = (bf16[64,10,1]{2,1,0:T(8,128)(2,1)S(1)}, bf16[64,10,1]{2,1,0:T(8,128)(2,1)S(1)}, u32[]{:S(2)}, u32[]{:S(2)}) collective-permute-start(bf16[64,10,1]{2,1,0:T(8,128)(2,1)S(1)} %get-tuple-element.158), channel_id=1, source_target_pairs={{0,1},{1,2},{2,3},{3,4},{4,5},{5,6},{6,7},{8,9},{9,10},{10,11},{11... | collective-permute-start | bytes 3848 | tf_op jit(solution)/shard_map/ppermute | solution.py:17
  312.0 10.1 %collective-permute-start.41 = (bf16[64,10,1]{2,1,0:T(8,128)(2,1)S(1)}, bf16[64,10,1]{2,1,0:T(8,128)(2,1)S(1)}, u32[]{:S(2)}, u32[]{:S(2)}) collective-permute-start(bf16[64,10,1]{2,1,0:T(8,128)(2,1)S(1)} %get-tuple-element.157), channel_id=1, source_target_pairs={{1,0},{2,1},{3,2},{4,3},{5,4},{6,5},{7,6},{9,8},{10,9},{11,10},{12... | collective-permute-start | bytes 3848 | tf_op jit(solution)/shard_map/ppermute | solution.py:19
  331.8 8.0 %collective-permute-start.44 = (bf16[64,10,1]{2,1,0:T(8,128)(2,1)S(1)}, bf16[64,10,1]{2,1,0:T(8,128)(2,1)S(1)}, u32[]{:S(2)}, u32[]{:S(2)}) collective-permute-start(bf16[64,10,1]{2,1,0:T(8,128)(2,1)S(1)} %get-tuple-element.156), channel_id=1, source_target_pairs={{0,1},{1,2},{2,3},{3,4},{4,5},{5,6},{6,7},{8,9},{9,10},{10,11},{11... | collective-permute-start | bytes 3848 | tf_op jit(solution)/shard_map/ppermute | solution.py:17
  335.4 9.0 %collective-permute-start.45 = (bf16[64,10,1]{2,1,0:T(8,128)(2,1)S(1)}, bf16[64,10,1]{2,1,0:T(8,128)(2,1)S(1)}, u32[]{:S(2)}, u32[]{:S(2)}) collective-permute-start(bf16[64,10,1]{2,1,0:T(8,128)(2,1)S(1)} %get-tuple-element.155), channel_id=1, source_target_pairs={{1,0},{2,1},{3,2},{4,3},{5,4},{6,5},{7,6},{9,8},{10,9},{11,10},{12... | collective-permute-start | bytes 3848 | tf_op jit(solution)/shard_map/ppermute | solution.py:19
  354.0 7.8 %collective-permute-start.48 = (bf16[64,10,1]{2,1,0:T(8,128)(2,1)S(1)}, bf16[64,10,1]{2,1,0:T(8,128)(2,1)S(1)}, u32[]{:S(2)}, u32[]{:S(2)}) collective-permute-start(bf16[64,10,1]{2,1,0:T(8,128)(2,1)S(1)} %get-tuple-element.154), channel_id=1, source_target_pairs={{0,1},{1,2},{2,3},{3,4},{4,5},{5,6},{6,7},{8,9},{9,10},{10,11},{11... | collective-permute-start | bytes 3848 | tf_op jit(solution)/shard_map/ppermute | solution.py:17
  357.8 9.0 %collective-permute-start.49 = (bf16[64,10,1]{2,1,0:T(8,128)(2,1)S(1)}, bf16[64,10,1]{2,1,0:T(8,128)(2,1)S(1)}, u32[]{:S(2)}, u32[]{:S(2)}) collective-permute-start(bf16[64,10,1]{2,1,0:T(8,128)(2,1)S(1)} %get-tuple-element.153), channel_id=1, source_target_pairs={{1,0},{2,1},{3,2},{4,3},{5,4},{6,5},{7,6},{9,8},{10,9},{11,10},{12... | collective-permute-start | bytes 3848 | tf_op jit(solution)/shard_map/ppermute | solution.py:19
  369.6 11.9 %collective-permute-start.1 = (f32[64,1024]{1,0:T(8,128)S(1)}, f32[64,1024]{1,0:T(8,128)S(1)}, u32[]{:S(2)}, u32[]{:S(2)}) collective-permute-start(f32[64,1024]{1,0:T(8,128)S(1)} %convolution_add_fusion.5), channel_id=1, source_target_pairs={{64,0},{128,64},{192,128},{256,192},{320,256},{384,320},{448,384},... | collective-permute-start | bytes 786440 | tf_op jit(solution)/shard_map/while/body/eval_jaxpr/ppermute | solution.py:29
  381.9 12.0 %collective-permute-start.1 = (f32[64,1024]{1,0:T(8,128)S(1)}, f32[64,1024]{1,0:T(8,128)S(1)}, u32[]{:S(2)}, u32[]{:S(2)}) collective-permute-start(f32[64,1024]{1,0:T(8,128)S(1)} %convolution_add_fusion.5), channel_id=1, source_target_pairs={{64,0},{128,64},{192,128},{256,192},{320,256},{384,320},{448,384},... | collective-permute-start | bytes 786440 | tf_op jit(solution)/shard_map/while/body/eval_jaxpr/ppermute | solution.py:29
  394.3 11.4 %collective-permute-start.1 = (f32[64,1024]{1,0:T(8,128)S(1)}, f32[64,1024]{1,0:T(8,128)S(1)}, u32[]{:S(2)}, u32[]{:S(2)}) collective-permute-start(f32[64,1024]{1,0:T(8,128)S(1)} %convolution_add_fusion.5), channel_id=1, source_target_pairs={{64,0},{128,64},{192,128},{256,192},{320,256},{384,320},{448,384},... | collective-permute-start | bytes 786440 | tf_op jit(solution)/shard_map/while/body/eval_jaxpr/ppermute | solution.py:29
  406.0 10.3 %collective-permute-start.1 = (f32[64,1024]{1,0:T(8,128)S(1)}, f32[64,1024]{1,0:T(8,128)S(1)}, u32[]{:S(2)}, u32[]{:S(2)}) collective-permute-start(f32[64,1024]{1,0:T(8,128)S(1)} %convolution_add_fusion.5), channel_id=1, source_target_pairs={{64,0},{128,64},{192,128},{256,192},{320,256},{384,320},{448,384},... | collective-permute-start | bytes 786440 | tf_op jit(solution)/shard_map/while/body/eval_jaxpr/ppermute | solution.py:29
  416.7 7.7 %collective-permute-start.1 = (f32[64,1024]{1,0:T(8,128)S(1)}, f32[64,1024]{1,0:T(8,128)S(1)}, u32[]{:S(2)}, u32[]{:S(2)}) collective-permute-start(f32[64,1024]{1,0:T(8,128)S(1)} %convolution_add_fusion.5), channel_id=1, source_target_pairs={{64,0},{128,64},{192,128},{256,192},{320,256},{384,320},{448,384},... | collective-permute-start | bytes 786440 | tf_op jit(solution)/shard_map/while/body/eval_jaxpr/ppermute | solution.py:29
  424.8 7.1 %collective-permute-start.1 = (f32[64,1024]{1,0:T(8,128)S(1)}, f32[64,1024]{1,0:T(8,128)S(1)}, u32[]{:S(2)}, u32[]{:S(2)}) collective-permute-start(f32[64,1024]{1,0:T(8,128)S(1)} %convolution_add_fusion.5), channel_id=1, source_target_pairs={{64,0},{128,64},{192,128},{256,192},{320,256},{384,320},{448,384},... | collective-permute-start | bytes 786440 | tf_op jit(solution)/shard_map/while/body/eval_jaxpr/ppermute | solution.py:29
  432.2 8.1 %collective-permute-start.1 = (f32[64,1024]{1,0:T(8,128)S(1)}, f32[64,1024]{1,0:T(8,128)S(1)}, u32[]{:S(2)}, u32[]{:S(2)}) collective-permute-start(f32[64,1024]{1,0:T(8,128)S(1)} %convolution_add_fusion.5), channel_id=1, source_target_pairs={{64,0},{128,64},{192,128},{256,192},{320,256},{384,320},{448,384},... | collective-permute-start | bytes 786440 | tf_op jit(solution)/shard_map/while/body/eval_jaxpr/ppermute | solution.py:29
  (42 other events, 237.3 us)
Sparse Core Ops, SparseCore 0:
  357.9 193.3 all-reduce.1
where the time goes:
time: 563 us; the launch traced here: 560 us
  waiting for transfers between devices  312 us (55%)
  starting transfers between devices  164 us (29%)
  local copies, waits for them, and re-layouts  28.5 us (5%)
  other arithmetic  24.9 us (4%)
  between operations  16.1 us (3%)
  matrix products  13.7 us (2%)
    psum x1, waiting for transfers between devices, local(): weight_grads = lax.psum(jnp.stack(grad_list, 0), ('row', 'col'))  110 us
    ppermute x14, waiting for transfers between devices, from_behind(): return lax.ppermute(array, axis, pairs)  88.8 us
    ppermute x24, waiting for transfers between devices, with_halo(): lax.ppermute(head, axis, [((i + 1) % count, i) for i in range(ends)])  78.5 us
    ppermute x24, starting transfers between devices, with_halo(): lax.ppermute(tail, axis, [(i, (i + 1) % count) for i in range(ends)])  77.9 us
    ppermute x24, starting transfers between devices, with_halo(): lax.ppermute(head, axis, [((i + 1) % count, i) for i in range(ends)])  45.4 us
    ppermute x14, starting transfers between devices, from_behind(): return lax.ppermute(array, axis, pairs)  41.1 us
    ppermute x24, waiting for transfers between devices, with_halo(): lax.ppermute(tail, axis, [(i, (i + 1) % count) for i in range(ends)])  34.7 us
    concatenate x36, other arithmetic, with_halo(): jnp.concatenate([lax.ppermute(tail, axis, [(i, (i + 1) % count) for i in...  21.9 us
  transfers between devices with their start and end apart: 63, of which 49 were waited for; matrix products, arithmetic and copies ran while one was open for 5% of the time, Pallas kernels for 0%

commit v1 on v0

--- a/solution.py
+++ b/solution.py
@@ -116,7 +116,7 @@
             preferred_element_type=jnp.float32,
         )
         adjoint = adjoint + back
-    weight_grads = lax.psum(jnp.stack(grad_list, 0), ("row", "col"))
+    weight_grads = jnp.sum(lax.all_gather(jnp.stack(grad_list, 0), ("row", "col")), axis=0)
     transposed = coarse_map.T
     back_map = jnp.where(is_last, zero_map, transposed)
     back_offset = jnp.where(is_last, adjoint, adjoint - exact_dot(transposed, guess_flat))

time: 563 us -> 535 us (0.950)
  waiting for transfers between devices: 312 us -> 261 us
  other arithmetic: 24.9 us -> 40.9 us
  starting transfers between devices: 164 us -> 176 us
    psum x1 -> x0, waiting for transfers between devices: 110 us -> none  [local(): weight_grads = lax.psum(jnp.stack(grad_list, 0), ('row', 'col'))]
    all_gather x0 -> x1, waiting for transfers between devices: none -> 72.2 us  [local(): lax.all_gather(jnp.stack(grad_list, 0), ('row', 'col'))]
    ppermute x24, waiting for transfers between devices: 78.5 us -> 48.1 us  [with_halo(): lax.ppermute(head, axis, [((i + 1) % count, i) for i in range(ends)])]
    reduce_sum x0 -> x1, other arithmetic: none -> 16.1 us  [local(): jnp.sum(lax.all_gather(jnp.stack(grad_list, 0), ('row', 'col')), axis=0)]
    ppermute x24, waiting for transfers between devices: 34.7 us -> 47.2 us  [with_halo(): lax.ppermute(tail, axis, [(i, (i + 1) % count) for i in range(ends)])]
    ppermute x24, starting transfers between devices: 45.4 us -> 54.4 us  [with_halo(): lax.ppermute(head, axis, [((i + 1) % count, i) for i in range(ends)])]
    unnamed x163 -> x158, local copies, waits for them, and re-layouts: 13.8 us -> 12.3 us
  transfers between devices with their start and end apart: 63 -> 63, of which waited for: 49 -> 50; matrix products, arithmetic and copies ran while one was open for 5% -> 5% of each run, Pallas kernels for 0% -> 0%
where the time goes in v1:
time: 535 us; the launch traced here: 532 us
  waiting for transfers between devices  261 us (49%)
  starting transfers between devices  176 us (33%)
  other arithmetic  40.9 us (8%)
  local copies, waits for them, and re-layouts  24.6 us (5%)
  between operations  16.1 us (3%)
  matrix products  12.9 us (2%)
    ppermute x14, waiting for transfers between devices, from_behind(): return lax.ppermute(array, axis, pairs)  93.2 us
    ppermute x24, starting transfers between devices, with_halo(): lax.ppermute(tail, axis, [(i, (i + 1) % count) for i in range(ends)])  79.6 us
    all_gather x1, waiting for transfers between devices, local(): lax.all_gather(jnp.stack(grad_list, 0), ('row', 'col'))  72.2 us
    ppermute x24, starting transfers between devices, with_halo(): lax.ppermute(head, axis, [((i + 1) % count, i) for i in range(ends)])  54.4 us
    ppermute x24, waiting for transfers between devices, with_halo(): lax.ppermute(head, axis, [((i + 1) % count, i) for i in range(ends)])  48.1 us
    ppermute x24, waiting for transfers between devices, with_halo(): lax.ppermute(tail, axis, [(i, (i + 1) % count) for i in range(ends)])  47.2 us
    ppermute x14, starting transfers between devices, from_behind(): return lax.ppermute(array, axis, pairs)  42.4 us
    concatenate x36, other arithmetic, with_halo(): jnp.concatenate([lax.ppermute(tail, axis, [(i, (i + 1) % count) for i in...  22.6 us
  transfers between devices with their start and end apart: 63, of which 50 were waited for; matrix products, arithmetic and copies ran while one was open for 5% of the time, Pallas kernels for 0%

profile of v1, /device:TPU:1, one launch (start us, length us, event | category | flops | bytes accessed | tf_op | source)
XLA Modules:
  0.0 532.1 jit_solution(7443753845258332755)
XLA Ops:
  8.2 8.8 %collective-permute-start.3 = (bf16[64,1,128]{2,1,0:T(2,128)(2,1)S(1)}, bf16[64,1,128]{2,1,0:T(2,128)(2,1)S(1)}, u32[]{:S(2)}, u32[]{:S(2)}) collective-permute-start(bf16[64,1,128]{2,1,0:T(2,128)(2,1)S(1)} %get-tuple-element.228), channel_id=1, source_target_pairs={{8,0},{16,8},{24,16},{32,24},{40,32},{48,40},{56,48},{9,1},{17,9},... | collective-permute-start | bytes 49160 | tf_op jit(solution)/shard_map/ppermute | solution.py:19
  23.0 4.4 collective-permute-done.4
  43.0 4.8 collective-permute-done.8
  55.5 3.7 collective-permute-start.10
  60.5 4.6 collective-permute-start.12
  70.6 4.7 collective-permute-done.13
  78.6 3.5 collective-permute-start.14
  84.1 3.6 collective-permute-start.16
  89.1 4.1 collective-permute-done.16
  93.8 3.9 collective-permute-done.17
  99.4 62.0 %while.20 = (s32[]{:T(128)}, f32[64,1024]{1,0:T(8,128)S(1)}, f32[64,64]{1,0:T(8,128)S(1)}, f32[64,1024]{1,0:T(8,128)S(1)}, s32[]{:T(128)}) while((s32[]{:T(128)}, f32[64,1024]{1,0:T(8,128)S(1)}, f32[64,64]{1,0:T(8,128)S(1)}, f32[64,1024]{1,0:T(8,128)S(1)}, s32[]{:T(128)}) %tuple.144), condition=%wide.region_2.3_spmd, body=%wide.region_1.2_spmd.sunk | while | flops 50397184 | bytes 1851493 | solution.py:91
  99.8 4.0 collective-permute-start
  103.8 5.3 collective-permute-done
  109.4 4.1 collective-permute-start
  113.5 4.3 collective-permute-done
  118.2 4.1 collective-permute-start
  126.0 5.0 collective-permute-start
  134.7 5.3 %collective-permute-start = (f32[64,1024]{1,0:T(8,128)S(1)}, f32[64,1024]{1,0:T(8,128)S(1)}, u32[]{:S(2)}, u32[]{:S(2)}) collective-permute-start(f32[64,1024]{1,0:T(8,128)S(1)} %convolution_add_fusion.4), channel_id=1, source_target_pairs={{0,64},{64,128},{128,192},{192,256},{256,320},{320,384},{384,448},... | collective-permute-start | bytes 786440 | tf_op jit(solution)/shard_map/while/body/eval_jaxpr/ppermute | solution.py:29
  143.7 5.3 %collective-permute-start = (f32[64,1024]{1,0:T(8,128)S(1)}, f32[64,1024]{1,0:T(8,128)S(1)}, u32[]{:S(2)}, u32[]{:S(2)}) collective-permute-start(f32[64,1024]{1,0:T(8,128)S(1)} %convolution_add_fusion.4), channel_id=1, source_target_pairs={{0,64},{64,128},{128,192},{192,256},{256,320},{320,384},{384,448},... | collective-permute-start | bytes 786440 | tf_op jit(solution)/shard_map/while/body/eval_jaxpr/ppermute | solution.py:29
  152.7 5.5 %collective-permute-start = (f32[64,1024]{1,0:T(8,128)S(1)}, f32[64,1024]{1,0:T(8,128)S(1)}, u32[]{:S(2)}, u32[]{:S(2)}) collective-permute-start(f32[64,1024]{1,0:T(8,128)S(1)} %convolution_add_fusion.4), channel_id=1, source_target_pairs={{0,64},{64,128},{128,192},{192,256},{256,320},{320,384},{384,448},... | collective-permute-start | bytes 786440 | tf_op jit(solution)/shard_map/while/body/eval_jaxpr/ppermute | solution.py:29
  161.6 8.4 %collective-permute-start.19 = (bf16[64,1,128]{2,1,0:T(2,128)(2,1)S(1)}, bf16[64,1,128]{2,1,0:T(2,128)(2,1)S(1)}, u32[]{:S(2)}, u32[]{:S(2)}) collective-permute-start(bf16[64,1,128]{2,1,0:T(2,128)(2,1)S(1)} %get-tuple-element.220), channel_id=1, source_target_pairs={{8,0},{16,8},{24,16},{32,24},{40,32},{48,40},{56,48},{9,1},{17,9},... | collective-permute-start | bytes 49160 | tf_op jit(solution)/shard_map/ppermute | solution.py:19
  170.0 7.0 %collective-permute-start.18 = (bf16[64,1,128]{2,1,0:T(2,128)(2,1)S(1)}, bf16[64,1,128]{2,1,0:T(2,128)(2,1)S(1)}, u32[]{:S(2)}, u32[]{:S(2)}) collective-permute-start(bf16[64,1,128]{2,1,0:T(2,128)(2,1)S(1)} %get-tuple-element.219), channel_id=1, source_target_pairs={{0,8},{8,16},{16,24},{24,32},{32,40},{40,48},{48,56},{1,9},{9,17},... | collective-permute-start | bytes 49160 | tf_op jit(solution)/shard_map/ppermute | solution.py:17
  183.7 3.5 collective-permute-done.21
  190.5 5.6 %collective-permute-start.22 = (bf16[64,1,128]{2,1,0:T(2,128)(2,1)S(1)}, bf16[64,1,128]{2,1,0:T(2,128)(2,1)S(1)}, u32[]{:S(2)}, u32[]{:S(2)}) collective-permute-start(bf16[64,1,128]{2,1,0:T(2,128)(2,1)S(1)} %get-tuple-element.217), channel_id=1, source_target_pairs={{0,8},{8,16},{16,24},{24,32},{32,40},{40,48},{48,56},{1,9},{9,17},... | collective-permute-start | bytes 49160 | tf_op jit(solution)/shard_map/ppermute | solution.py:17
  204.5 3.6 collective-permute-done.25
  212.1 5.2 collective-permute-start.26
  222.0 3.5 collective-permute-done.28
  226.1 3.6 collective-permute-done.29
  233.6 3.8 collective-permute-start.30
  240.1 3.9 collective-permute-start.32
  250.2 4.6 collective-permute-done.33
  259.7 3.9 collective-permute-start.34
  276.3 5.2 collective-permute-done.37
  287.3 3.7 collective-permute-start.38
  300.2 3.9 collective-permute-done.40
  323.5 3.8 collective-permute-done.44
  327.7 4.1 collective-permute-done.45
  351.0 4.6 collective-permute-done.49
  357.3 78.9 %while.21 = (s32[]{:T(128)}, f32[64,1024]{1,0:T(8,128)S(1)}, f32[64,64]{1,0:T(8,128)S(1)}, f32[64,1024]{1,0:T(8,128)S(1)}, s32[]{:T(128)}) while((s32[]{:T(128)}, f32[64,1024]{1,0:T(8,128)S(1)}, f32[64,64]{1,0:T(8,128)S(1)}, f32[64,1024]{1,0:T(8,128)S(1)}, s32[]{:T(128)}) %tuple.147), condition=%wide.region_4.5_spmd, body=%wide.region_3.4_spmd.sunk | while | flops 50397184 | bytes 1851493 | solution.py:127
  358.9 10.3 %collective-permute-done.1 = f32[64,1024]{1,0:T(8,128)S(1)} collective-permute-done((f32[64,1024]{1,0:T(8,128)S(1)}, f32[64,1024]{1,0:T(8,128)S(1)}, u32[]{:S(2)}, u32[]{:S(2)}) %collective-permute-start.1) | collective-permute-done | bytes 262176 | tf_op jit(solution)/shard_map/while/body/eval_jaxpr/ppermute | solution.py:29
  370.9 13.5 %collective-permute-done.1 = f32[64,1024]{1,0:T(8,128)S(1)} collective-permute-done((f32[64,1024]{1,0:T(8,128)S(1)}, f32[64,1024]{1,0:T(8,128)S(1)}, u32[]{:S(2)}, u32[]{:S(2)}) %collective-permute-start.1) | collective-permute-done | bytes 262176 | tf_op jit(solution)/shard_map/while/body/eval_jaxpr/ppermute | solution.py:29
  386.1 12.2 %collective-permute-done.1 = f32[64,1024]{1,0:T(8,128)S(1)} collective-permute-done((f32[64,1024]{1,0:T(8,128)S(1)}, f32[64,1024]{1,0:T(8,128)S(1)}, u32[]{:S(2)}, u32[]{:S(2)}) %collective-permute-start.1) | collective-permute-done | bytes 262176 | tf_op jit(solution)/shard_map/while/body/eval_jaxpr/ppermute | solution.py:29
  399.9 10.6 %collective-permute-done.1 = f32[64,1024]{1,0:T(8,128)S(1)} collective-permute-done((f32[64,1024]{1,0:T(8,128)S(1)}, f32[64,1024]{1,0:T(8,128)S(1)}, u32[]{:S(2)}, u32[]{:S(2)}) %collective-permute-start.1) | collective-permute-done | bytes 262176 | tf_op jit(solution)/shard_map/while/body/eval_jaxpr/ppermute | solution.py:29
  412.1 7.3 %collective-permute-done.1 = f32[64,1024]{1,0:T(8,128)S(1)} collective-permute-done((f32[64,1024]{1,0:T(8,128)S(1)}, f32[64,1024]{1,0:T(8,128)S(1)}, u32[]{:S(2)}, u32[]{:S(2)}) %collective-permute-start.1) | collective-permute-done | bytes 262176 | tf_op jit(solution)/shard_map/while/body/eval_jaxpr/ppermute | solution.py:29
  421.1 6.5 %collective-permute-done.1 = f32[64,1024]{1,0:T(8,128)S(1)} collective-permute-done((f32[64,1024]{1,0:T(8,128)S(1)}, f32[64,1024]{1,0:T(8,128)S(1)}, u32[]{:S(2)}, u32[]{:S(2)}) %collective-permute-start.1) | collective-permute-done | bytes 262176 | tf_op jit(solution)/shard_map/while/body/eval_jaxpr/ppermute | solution.py:29
  429.3 6.9 %collective-permute-done.1 = f32[64,1024]{1,0:T(8,128)S(1)} collective-permute-done((f32[64,1024]{1,0:T(8,128)S(1)}, f32[64,1024]{1,0:T(8,128)S(1)}, u32[]{:S(2)}, u32[]{:S(2)}) %collective-permute-start.1) | collective-permute-done | bytes 262176 | tf_op jit(solution)/shard_map/while/body/eval_jaxpr/ppermute | solution.py:29
  437.0 72.2 %all-gather.3.cloned.1.call-done = f32[256,64,576]{2,1,0:T(8,128)} async-done(((f32[4,64,576]{2,1,0:T(8,128)}), f32[256,64,576]{2,1,0:T(8,128)}) %all-gather.3.cloned.1.call-update) | async-done | bytes 37748752 | tf_op jit(solution)/shard_map/all_gather | solution.py:119
  509.2 16.1 %reduce_sum.19 = f32[4,64,576]{2,1,0:T(8,128)} reduce(f32[64,4,64,576]{3,2,1,0:T(8,128)} %bitcast.508, f32[]{:T(128)} %constant.4.clone.1), dimensions={0}, to_apply=%region_5.6 | reduce | flops 9289728 | bytes 38338564 | tf_op jit(solution)/shard_map/reduce_sum | solution.py:119
  (372 shorter events, 189.3 us)
Async XLA Ops:
  7.2 502.0 %all-gather.3.cloned.1.call-start = ((), (), s32[]{:S(2)}) async-start(), calls=%async_computation | async-start | bytes 42598400 | tf_op jit(solution)/shard_map/all_gather | solution.py:119
  8.2 10.7 %collective-permute-start.3 = (bf16[64,1,128]{2,1,0:T(2,128)(2,1)S(1)}, bf16[64,1,128]{2,1,0:T(2,128)(2,1)S(1)}, u32[]{:S(2)}, u32[]{:S(2)}) collective-permute-start(bf16[64,1,128]{2,1,0:T(2,128)(2,1)S(1)} %get-tuple-element.228), channel_id=1, source_target_pairs={{8,0},{16,8},{24,16},{32,24},{40,32},{48,40},{56,48},{9,1},{17,9},... | collective-permute-start | bytes 49160 | tf_op jit(solution)/shard_map/ppermute | solution.py:19
  20.4 7.1 %collective-permute-start.4 = (bf16[64,10,1]{2,1,0:T(8,128)(2,1)S(1)}, bf16[64,10,1]{2,1,0:T(8,128)(2,1)S(1)}, u32[]{:S(2)}, u32[]{:S(2)}) collective-permute-start(bf16[64,10,1]{2,1,0:T(8,128)(2,1)S(1)} %get-tuple-element.180), channel_id=1, source_target_pairs={{0,1},{1,2},{2,3},{3,4},{4,5},{5,6},{6,7},{8,9},{9,10},{10,11},{11... | collective-permute-start | bytes 3848 | tf_op jit(solution)/shard_map/ppermute | solution.py:17
  21.7 9.6 %collective-permute-start.5 = (bf16[64,10,1]{2,1,0:T(8,128)(2,1)S(1)}, bf16[64,10,1]{2,1,0:T(8,128)(2,1)S(1)}, u32[]{:S(2)}, u32[]{:S(2)}) collective-permute-start(bf16[64,10,1]{2,1,0:T(8,128)(2,1)S(1)} %get-tuple-element.179), channel_id=1, source_target_pairs={{1,0},{2,1},{3,2},{4,3},{5,4},{6,5},{7,6},{9,8},{10,9},{11,10},{12... | collective-permute-start | bytes 3848 | tf_op jit(solution)/shard_map/ppermute | solution.py:19
  40.4 7.4 %collective-permute-start.8 = (bf16[64,10,1]{2,1,0:T(8,128)(2,1)S(1)}, bf16[64,10,1]{2,1,0:T(8,128)(2,1)S(1)}, u32[]{:S(2)}, u32[]{:S(2)}) collective-permute-start(bf16[64,10,1]{2,1,0:T(8,128)(2,1)S(1)} %get-tuple-element.178), channel_id=1, source_target_pairs={{0,1},{1,2},{2,3},{3,4},{4,5},{5,6},{6,7},{8,9},{9,10},{10,11},{11... | collective-permute-start | bytes 3848 | tf_op jit(solution)/shard_map/ppermute | solution.py:17
  41.7 10.1 %collective-permute-start.9 = (bf16[64,10,1]{2,1,0:T(8,128)(2,1)S(1)}, bf16[64,10,1]{2,1,0:T(8,128)(2,1)S(1)}, u32[]{:S(2)}, u32[]{:S(2)}) collective-permute-start(bf16[64,10,1]{2,1,0:T(8,128)(2,1)S(1)} %get-tuple-element.177), channel_id=1, source_target_pairs={{1,0},{2,1},{3,2},{4,3},{5,4},{6,5},{7,6},{9,8},{10,9},{11,10},{12... | collective-permute-start | bytes 3848 | tf_op jit(solution)/shard_map/ppermute | solution.py:19
  60.5 9.6 %collective-permute-start.12 = (bf16[64,10,1]{2,1,0:T(8,128)(2,1)S(1)}, bf16[64,10,1]{2,1,0:T(8,128)(2,1)S(1)}, u32[]{:S(2)}, u32[]{:S(2)}) collective-permute-start(bf16[64,10,1]{2,1,0:T(8,128)(2,1)S(1)} %get-tuple-element.176), channel_id=1, source_target_pairs={{0,1},{1,2},{2,3},{3,4},{4,5},{5,6},{6,7},{8,9},{9,10},{10,11},{11... | collective-permute-start | bytes 3848 | tf_op jit(solution)/shard_map/ppermute | solution.py:17
  65.9 9.3 %collective-permute-start.13 = (bf16[64,10,1]{2,1,0:T(8,128)(2,1)S(1)}, bf16[64,10,1]{2,1,0:T(8,128)(2,1)S(1)}, u32[]{:S(2)}, u32[]{:S(2)}) collective-permute-start(bf16[64,10,1]{2,1,0:T(8,128)(2,1)S(1)} %get-tuple-element.175), channel_id=1, source_target_pairs={{1,0},{2,1},{3,2},{4,3},{5,4},{6,5},{7,6},{9,8},{10,9},{11,10},{12... | collective-permute-start | bytes 3848 | tf_op jit(solution)/shard_map/ppermute | solution.py:19
  84.1 9.2 %collective-permute-start.16 = (bf16[64,10,1]{2,1,0:T(8,128)(2,1)S(1)}, bf16[64,10,1]{2,1,0:T(8,128)(2,1)S(1)}, u32[]{:S(2)}, u32[]{:S(2)}) collective-permute-start(bf16[64,10,1]{2,1,0:T(8,128)(2,1)S(1)} %get-tuple-element.174), channel_id=1, source_target_pairs={{0,1},{1,2},{2,3},{3,4},{4,5},{5,6},{6,7},{8,9},{9,10},{10,11},{11... | collective-permute-start | bytes 3848 | tf_op jit(solution)/shard_map/ppermute | solution.py:17
  87.8 9.8 %collective-permute-start.17 = (bf16[64,10,1]{2,1,0:T(8,128)(2,1)}, bf16[64,10,1]{2,1,0:T(8,128)(2,1)S(1)}, u32[]{:S(2)}, u32[]{:S(2)}) collective-permute-start(bf16[64,10,1]{2,1,0:T(8,128)(2,1)} %get-tuple-element.173), channel_id=1, source_target_pairs={{1,0},{2,1},{3,2},{4,3},{5,4},{6,5},{7,6},{9,8},{10,9},{11,10},{12... | collective-permute-start | bytes 3848 | tf_op jit(solution)/shard_map/ppermute | solution.py:19
  99.8 9.3 %collective-permute-start = (f32[64,1024]{1,0:T(8,128)S(1)}, f32[64,1024]{1,0:T(8,128)S(1)}, u32[]{:S(2)}, u32[]{:S(2)}) collective-permute-start(f32[64,1024]{1,0:T(8,128)S(1)} %convolution_add_fusion.4), channel_id=1, source_target_pairs={{0,64},{64,128},{128,192},{192,256},{256,320},{320,384},{384,448},... | collective-permute-start | bytes 786440 | tf_op jit(solution)/shard_map/while/body/eval_jaxpr/ppermute | solution.py:29
  109.4 8.4 %collective-permute-start = (f32[64,1024]{1,0:T(8,128)S(1)}, f32[64,1024]{1,0:T(8,128)S(1)}, u32[]{:S(2)}, u32[]{:S(2)}) collective-permute-start(f32[64,1024]{1,0:T(8,128)S(1)} %convolution_add_fusion.4), channel_id=1, source_target_pairs={{0,64},{64,128},{128,192},{192,256},{256,320},{320,384},{384,448},... | collective-permute-start | bytes 786440 | tf_op jit(solution)/shard_map/while/body/eval_jaxpr/ppermute | solution.py:29
  118.2 7.4 %collective-permute-start = (f32[64,1024]{1,0:T(8,128)S(1)}, f32[64,1024]{1,0:T(8,128)S(1)}, u32[]{:S(2)}, u32[]{:S(2)}) collective-permute-start(f32[64,1024]{1,0:T(8,128)S(1)} %convolution_add_fusion.4), channel_id=1, source_target_pairs={{0,64},{64,128},{128,192},{192,256},{256,320},{320,384},{384,448},... | collective-permute-start | bytes 786440 | tf_op jit(solution)/shard_map/while/body/eval_jaxpr/ppermute | solution.py:29
  126.0 8.3 %collective-permute-start = (f32[64,1024]{1,0:T(8,128)S(1)}, f32[64,1024]{1,0:T(8,128)S(1)}, u32[]{:S(2)}, u32[]{:S(2)}) collective-permute-start(f32[64,1024]{1,0:T(8,128)S(1)} %convolution_add_fusion.4), channel_id=1, source_target_pairs={{0,64},{64,128},{128,192},{192,256},{256,320},{320,384},{384,448},... | collective-permute-start | bytes 786440 | tf_op jit(solution)/shard_map/while/body/eval_jaxpr/ppermute | solution.py:29
  134.7 8.6 %collective-permute-start = (f32[64,1024]{1,0:T(8,128)S(1)}, f32[64,1024]{1,0:T(8,128)S(1)}, u32[]{:S(2)}, u32[]{:S(2)}) collective-permute-start(f32[64,1024]{1,0:T(8,128)S(1)} %convolution_add_fusion.4), channel_id=1, source_target_pairs={{0,64},{64,128},{128,192},{192,256},{256,320},{320,384},{384,448},... | collective-permute-start | bytes 786440 | tf_op jit(solution)/shard_map/while/body/eval_jaxpr/ppermute | solution.py:29
  143.7 8.6 %collective-permute-start = (f32[64,1024]{1,0:T(8,128)S(1)}, f32[64,1024]{1,0:T(8,128)S(1)}, u32[]{:S(2)}, u32[]{:S(2)}) collective-permute-start(f32[64,1024]{1,0:T(8,128)S(1)} %convolution_add_fusion.4), channel_id=1, source_target_pairs={{0,64},{64,128},{128,192},{192,256},{256,320},{320,384},{384,448},... | collective-permute-start | bytes 786440 | tf_op jit(solution)/shard_map/while/body/eval_jaxpr/ppermute | solution.py:29
  152.7 8.8 %collective-permute-start = (f32[64,1024]{1,0:T(8,128)S(1)}, f32[64,1024]{1,0:T(8,128)S(1)}, u32[]{:S(2)}, u32[]{:S(2)}) collective-permute-start(f32[64,1024]{1,0:T(8,128)S(1)} %convolution_add_fusion.4), channel_id=1, source_target_pairs={{0,64},{64,128},{128,192},{192,256},{256,320},{320,384},{384,448},... | collective-permute-start | bytes 786440 | tf_op jit(solution)/shard_map/while/body/eval_jaxpr/ppermute | solution.py:29
  161.6 15.4 %collective-permute-start.19 = (bf16[64,1,128]{2,1,0:T(2,128)(2,1)S(1)}, bf16[64,1,128]{2,1,0:T(2,128)(2,1)S(1)}, u32[]{:S(2)}, u32[]{:S(2)}) collective-permute-start(bf16[64,1,128]{2,1,0:T(2,128)(2,1)S(1)} %get-tuple-element.220), channel_id=1, source_target_pairs={{8,0},{16,8},{24,16},{32,24},{40,32},{48,40},{56,48},{9,1},{17,9},... | collective-permute-start | bytes 49160 | tf_op jit(solution)/shard_map/ppermute | solution.py:19
  170.0 8.0 %collective-permute-start.18 = (bf16[64,1,128]{2,1,0:T(2,128)(2,1)S(1)}, bf16[64,1,128]{2,1,0:T(2,128)(2,1)S(1)}, u32[]{:S(2)}, u32[]{:S(2)}) collective-permute-start(bf16[64,1,128]{2,1,0:T(2,128)(2,1)S(1)} %get-tuple-element.219), channel_id=1, source_target_pairs={{0,8},{8,16},{16,24},{24,32},{32,40},{40,48},{48,56},{1,9},{9,17},... | collective-permute-start | bytes 49160 | tf_op jit(solution)/shard_map/ppermute | solution.py:17
  179.9 7.3 %collective-permute-start.21 = (bf16[64,10,1]{2,1,0:T(8,128)(2,1)S(1)}, bf16[64,10,1]{2,1,0:T(8,128)(2,1)S(1)}, u32[]{:S(2)}, u32[]{:S(2)}) collective-permute-start(bf16[64,10,1]{2,1,0:T(8,128)(2,1)S(1)} %get-tuple-element.171), channel_id=1, source_target_pairs={{1,0},{2,1},{3,2},{4,3},{5,4},{6,5},{7,6},{9,8},{10,9},{11,10},{12... | collective-permute-start | bytes 3848 | tf_op jit(solution)/shard_map/ppermute | solution.py:19
  188.6 7.5 %collective-permute-start.23 = (bf16[64,1,128]{2,1,0:T(2,128)(2,1)S(1)}, bf16[64,1,128]{2,1,0:T(2,128)(2,1)S(1)}, u32[]{:S(2)}, u32[]{:S(2)}) collective-permute-start(bf16[64,1,128]{2,1,0:T(2,128)(2,1)S(1)} %get-tuple-element.218), channel_id=1, source_target_pairs={{8,0},{16,8},{24,16},{32,24},{40,32},{48,40},{56,48},{9,1},{17,9},... | collective-permute-start | bytes 49160 | tf_op jit(solution)/shard_map/ppermute | solution.py:19
  190.5 6.6 %collective-permute-start.22 = (bf16[64,1,128]{2,1,0:T(2,128)(2,1)S(1)}, bf16[64,1,128]{2,1,0:T(2,128)(2,1)S(1)}, u32[]{:S(2)}, u32[]{:S(2)}) collective-permute-start(bf16[64,1,128]{2,1,0:T(2,128)(2,1)S(1)} %get-tuple-element.217), channel_id=1, source_target_pairs={{0,8},{8,16},{16,24},{24,32},{32,40},{40,48},{48,56},{1,9},{9,17},... | collective-permute-start | bytes 49160 | tf_op jit(solution)/shard_map/ppermute | solution.py:17
  197.4 6.6 %collective-permute-start.24 = (bf16[64,10,1]{2,1,0:T(8,128)(2,1)S(1)}, bf16[64,10,1]{2,1,0:T(8,128)(2,1)S(1)}, u32[]{:S(2)}, u32[]{:S(2)}) collective-permute-start(bf16[64,10,1]{2,1,0:T(8,128)(2,1)S(1)} %get-tuple-element.170), channel_id=1, source_target_pairs={{0,1},{1,2},{2,3},{3,4},{4,5},{5,6},{6,7},{8,9},{9,10},{10,11},{11... | collective-permute-start | bytes 3848 | tf_op jit(solution)/shard_map/ppermute | solution.py:17
  200.5 7.6 %collective-permute-start.25 = (bf16[64,10,1]{2,1,0:T(8,128)(2,1)S(1)}, bf16[64,10,1]{2,1,0:T(8,128)(2,1)S(1)}, u32[]{:S(2)}, u32[]{:S(2)}) collective-permute-start(bf16[64,10,1]{2,1,0:T(8,128)(2,1)S(1)} %get-tuple-element.169), channel_id=1, source_target_pairs={{1,0},{2,1},{3,2},{4,3},{5,4},{6,5},{7,6},{9,8},{10,9},{11,10},{12... | collective-permute-start | bytes 3848 | tf_op jit(solution)/shard_map/ppermute | solution.py:19
  210.2 7.1 %collective-permute-start.27 = (bf16[64,1,128]{2,1,0:T(2,128)(2,1)S(1)}, bf16[64,1,128]{2,1,0:T(2,128)(2,1)S(1)}, u32[]{:S(2)}, u32[]{:S(2)}) collective-permute-start(bf16[64,1,128]{2,1,0:T(2,128)(2,1)S(1)} %get-tuple-element.216), channel_id=1, source_target_pairs={{8,0},{16,8},{24,16},{32,24},{40,32},{48,40},{56,48},{9,1},{17,9},... | collective-permute-start | bytes 49160 | tf_op jit(solution)/shard_map/ppermute | solution.py:19
  212.1 6.2 %collective-permute-start.26 = (bf16[64,1,128]{2,1,0:T(2,128)(2,1)S(1)}, bf16[64,1,128]{2,1,0:T(2,128)(2,1)S(1)}, u32[]{:S(2)}, u32[]{:S(2)}) collective-permute-start(bf16[64,1,128]{2,1,0:T(2,128)(2,1)S(1)} %get-tuple-element.215), channel_id=1, source_target_pairs={{0,8},{8,16},{16,24},{24,32},{32,40},{40,48},{48,56},{1,9},{9,17},... | collective-permute-start | bytes 49160 | tf_op jit(solution)/shard_map/ppermute | solution.py:17
  218.6 7.0 %collective-permute-start.28 = (bf16[64,10,1]{2,1,0:T(8,128)(2,1)S(1)}, bf16[64,10,1]{2,1,0:T(8,128)(2,1)S(1)}, u32[]{:S(2)}, u32[]{:S(2)}) collective-permute-start(bf16[64,10,1]{2,1,0:T(8,128)(2,1)S(1)} %get-tuple-element.168), channel_id=1, source_target_pairs={{0,1},{1,2},{2,3},{3,4},{4,5},{5,6},{6,7},{8,9},{9,10},{10,11},{11... | collective-permute-start | bytes 3848 | tf_op jit(solution)/shard_map/ppermute | solution.py:17
  220.7 9.0 %collective-permute-start.29 = (bf16[64,10,1]{2,1,0:T(8,128)(2,1)S(1)}, bf16[64,10,1]{2,1,0:T(8,128)(2,1)S(1)}, u32[]{:S(2)}, u32[]{:S(2)}) collective-permute-start(bf16[64,10,1]{2,1,0:T(8,128)(2,1)S(1)} %get-tuple-element.167), channel_id=1, source_target_pairs={{1,0},{2,1},{3,2},{4,3},{5,4},{6,5},{7,6},{9,8},{10,9},{11,10},{12... | collective-permute-start | bytes 3848 | tf_op jit(solution)/shard_map/ppermute | solution.py:19
  240.1 8.3 %collective-permute-start.32 = (bf16[64,10,1]{2,1,0:T(8,128)(2,1)}, bf16[64,10,1]{2,1,0:T(8,128)(2,1)}, u32[]{:S(2)}, u32[]{:S(2)}) collective-permute-start(bf16[64,10,1]{2,1,0:T(8,128)(2,1)} %get-tuple-element.166), channel_id=1, source_target_pairs={{0,1},{1,2},{2,3},{3,4},{4,5},{5,6},{6,7},{8,9},{9,10},{10,11},{11... | collective-permute-start | bytes 3848 | tf_op jit(solution)/shard_map/ppermute | solution.py:17
  245.7 9.1 %collective-permute-start.33 = (bf16[64,10,1]{2,1,0:T(8,128)(2,1)}, bf16[64,10,1]{2,1,0:T(8,128)(2,1)S(1)}, u32[]{:S(2)}, u32[]{:S(2)}) collective-permute-start(bf16[64,10,1]{2,1,0:T(8,128)(2,1)} %get-tuple-element.165), channel_id=1, source_target_pairs={{1,0},{2,1},{3,2},{4,3},{5,4},{6,5},{7,6},{9,8},{10,9},{11,10},{12... | collective-permute-start | bytes 3848 | tf_op jit(solution)/shard_map/ppermute | solution.py:19
  257.8 6.9 %collective-permute-start.35 = (bf16[64,1,128]{2,1,0:T(2,128)(2,1)}, bf16[64,1,128]{2,1,0:T(2,128)(2,1)S(1)}, u32[]{:S(2)}, u32[]{:S(2)}) collective-permute-start(bf16[64,1,128]{2,1,0:T(2,128)(2,1)} %get-tuple-element.212), channel_id=1, source_target_pairs={{8,0},{16,8},{24,16},{32,24},{40,32},{48,40},{56,48},{9,1},{17,9},... | collective-permute-start | bytes 49160 | tf_op jit(solution)/shard_map/ppermute | solution.py:19
  266.7 7.9 %collective-permute-start.36 = (bf16[64,10,1]{2,1,0:T(8,128)(2,1)}, bf16[64,10,1]{2,1,0:T(8,128)(2,1)}, u32[]{:S(2)}, u32[]{:S(2)}) collective-permute-start(bf16[64,10,1]{2,1,0:T(8,128)(2,1)} %get-tuple-element.164), channel_id=1, source_target_pairs={{0,1},{1,2},{2,3},{3,4},{4,5},{5,6},{6,7},{8,9},{9,10},{10,11},{11... | collective-permute-start | bytes 3848 | tf_op jit(solution)/shard_map/ppermute | solution.py:17
  272.0 9.5 %collective-permute-start.37 = (bf16[64,10,1]{2,1,0:T(8,128)(2,1)}, bf16[64,10,1]{2,1,0:T(8,128)(2,1)S(1)}, u32[]{:S(2)}, u32[]{:S(2)}) collective-permute-start(bf16[64,10,1]{2,1,0:T(8,128)(2,1)} %get-tuple-element.163), channel_id=1, source_target_pairs={{1,0},{2,1},{3,2},{4,3},{5,4},{6,5},{7,6},{9,8},{10,9},{11,10},{12... | collective-permute-start | bytes 3848 | tf_op jit(solution)/shard_map/ppermute | solution.py:19
  285.2 9.9 %collective-permute-start.39 = (bf16[64,1,128]{2,1,0:T(2,128)(2,1)}, bf16[64,1,128]{2,1,0:T(2,128)(2,1)}, u32[]{:S(2)}, u32[]{:S(2)}) collective-permute-start(bf16[64,1,128]{2,1,0:T(2,128)(2,1)} %get-tuple-element.210), channel_id=1, source_target_pairs={{8,0},{16,8},{24,16},{32,24},{40,32},{48,40},{56,48},{9,1},{17,9},... | collective-permute-start | bytes 49160 | tf_op jit(solution)/shard_map/ppermute | solution.py:19
  287.3 7.8 %collective-permute-start.38 = (bf16[64,1,128]{2,1,0:T(2,128)(2,1)}, bf16[64,1,128]{2,1,0:T(2,128)(2,1)}, u32[]{:S(2)}, u32[]{:S(2)}) collective-permute-start(bf16[64,1,128]{2,1,0:T(2,128)(2,1)} %get-tuple-element.209), channel_id=1, source_target_pairs={{0,8},{8,16},{16,24},{24,32},{32,40},{40,48},{48,56},{1,9},{9,17},... | collective-permute-start | bytes 49160 | tf_op jit(solution)/shard_map/ppermute | solution.py:17
  296.3 7.9 %collective-permute-start.40 = (bf16[64,10,1]{2,1,0:T(8,128)(2,1)S(1)}, bf16[64,10,1]{2,1,0:T(8,128)(2,1)S(1)}, u32[]{:S(2)}, u32[]{:S(2)}) collective-permute-start(bf16[64,10,1]{2,1,0:T(8,128)(2,1)S(1)} %get-tuple-element.162), channel_id=1, source_target_pairs={{0,1},{1,2},{2,3},{3,4},{4,5},{5,6},{6,7},{8,9},{9,10},{10,11},{11... | collective-permute-start | bytes 3848 | tf_op jit(solution)/shard_map/ppermute | solution.py:17
  298.9 10.0 %collective-permute-start.41 = (bf16[64,10,1]{2,1,0:T(8,128)(2,1)S(1)}, bf16[64,10,1]{2,1,0:T(8,128)(2,1)S(1)}, u32[]{:S(2)}, u32[]{:S(2)}) collective-permute-start(bf16[64,10,1]{2,1,0:T(8,128)(2,1)S(1)} %get-tuple-element.161), channel_id=1, source_target_pairs={{1,0},{2,1},{3,2},{4,3},{5,4},{6,5},{7,6},{9,8},{10,9},{11,10},{12... | collective-permute-start | bytes 3848 | tf_op jit(solution)/shard_map/ppermute | solution.py:19
  319.0 8.2 %collective-permute-start.44 = (bf16[64,10,1]{2,1,0:T(8,128)(2,1)S(1)}, bf16[64,10,1]{2,1,0:T(8,128)(2,1)S(1)}, u32[]{:S(2)}, u32[]{:S(2)}) collective-permute-start(bf16[64,10,1]{2,1,0:T(8,128)(2,1)S(1)} %get-tuple-element.160), channel_id=1, source_target_pairs={{0,1},{1,2},{2,3},{3,4},{4,5},{5,6},{6,7},{8,9},{9,10},{10,11},{11... | collective-permute-start | bytes 3848 | tf_op jit(solution)/shard_map/ppermute | solution.py:17
  322.2 9.7 %collective-permute-start.45 = (bf16[64,10,1]{2,1,0:T(8,128)(2,1)S(1)}, bf16[64,10,1]{2,1,0:T(8,128)(2,1)S(1)}, u32[]{:S(2)}, u32[]{:S(2)}) collective-permute-start(bf16[64,10,1]{2,1,0:T(8,128)(2,1)S(1)} %get-tuple-element.159), channel_id=1, source_target_pairs={{1,0},{2,1},{3,2},{4,3},{5,4},{6,5},{7,6},{9,8},{10,9},{11,10},{12... | collective-permute-start | bytes 3848 | tf_op jit(solution)/shard_map/ppermute | solution.py:19
  342.3 8.2 %collective-permute-start.48 = (bf16[64,10,1]{2,1,0:T(8,128)(2,1)S(1)}, bf16[64,10,1]{2,1,0:T(8,128)(2,1)S(1)}, u32[]{:S(2)}, u32[]{:S(2)}) collective-permute-start(bf16[64,10,1]{2,1,0:T(8,128)(2,1)S(1)} %get-tuple-element.158), channel_id=1, source_target_pairs={{0,1},{1,2},{2,3},{3,4},{4,5},{5,6},{6,7},{8,9},{9,10},{10,11},{11... | collective-permute-start | bytes 3848 | tf_op jit(solution)/shard_map/ppermute | solution.py:17
  345.9 9.6 %collective-permute-start.49 = (bf16[64,10,1]{2,1,0:T(8,128)(2,1)S(1)}, bf16[64,10,1]{2,1,0:T(8,128)(2,1)S(1)}, u32[]{:S(2)}, u32[]{:S(2)}) collective-permute-start(bf16[64,10,1]{2,1,0:T(8,128)(2,1)S(1)} %get-tuple-element.157), channel_id=1, source_target_pairs={{1,0},{2,1},{3,2},{4,3},{5,4},{6,5},{7,6},{9,8},{10,9},{11,10},{12... | collective-permute-start | bytes 3848 | tf_op jit(solution)/shard_map/ppermute | solution.py:19
  357.6 11.6 %collective-permute-start.1 = (f32[64,1024]{1,0:T(8,128)S(1)}, f32[64,1024]{1,0:T(8,128)S(1)}, u32[]{:S(2)}, u32[]{:S(2)}) collective-permute-start(f32[64,1024]{1,0:T(8,128)S(1)} %convolution_add_fusion.5), channel_id=1, source_target_pairs={{64,0},{128,64},{192,128},{256,192},{320,256},{384,320},{448,384},... | collective-permute-start | bytes 786440 | tf_op jit(solution)/shard_map/while/body/eval_jaxpr/ppermute | solution.py:29
  369.6 14.8 %collective-permute-start.1 = (f32[64,1024]{1,0:T(8,128)S(1)}, f32[64,1024]{1,0:T(8,128)S(1)}, u32[]{:S(2)}, u32[]{:S(2)}) collective-permute-start(f32[64,1024]{1,0:T(8,128)S(1)} %convolution_add_fusion.5), channel_id=1, source_target_pairs={{64,0},{128,64},{192,128},{256,192},{320,256},{384,320},{448,384},... | collective-permute-start | bytes 786440 | tf_op jit(solution)/shard_map/while/body/eval_jaxpr/ppermute | solution.py:29
  384.8 13.5 %collective-permute-start.1 = (f32[64,1024]{1,0:T(8,128)S(1)}, f32[64,1024]{1,0:T(8,128)S(1)}, u32[]{:S(2)}, u32[]{:S(2)}) collective-permute-start(f32[64,1024]{1,0:T(8,128)S(1)} %convolution_add_fusion.5), channel_id=1, source_target_pairs={{64,0},{128,64},{192,128},{256,192},{320,256},{384,320},{448,384},... | collective-permute-start | bytes 786440 | tf_op jit(solution)/shard_map/while/body/eval_jaxpr/ppermute | solution.py:29
  398.6 11.9 %collective-permute-start.1 = (f32[64,1024]{1,0:T(8,128)S(1)}, f32[64,1024]{1,0:T(8,128)S(1)}, u32[]{:S(2)}, u32[]{:S(2)}) collective-permute-start(f32[64,1024]{1,0:T(8,128)S(1)} %convolution_add_fusion.5), channel_id=1, source_target_pairs={{64,0},{128,64},{192,128},{256,192},{320,256},{384,320},{448,384},... | collective-permute-start | bytes 786440 | tf_op jit(solution)/shard_map/while/body/eval_jaxpr/ppermute | solution.py:29
  410.8 8.6 %collective-permute-start.1 = (f32[64,1024]{1,0:T(8,128)S(1)}, f32[64,1024]{1,0:T(8,128)S(1)}, u32[]{:S(2)}, u32[]{:S(2)}) collective-permute-start(f32[64,1024]{1,0:T(8,128)S(1)} %convolution_add_fusion.5), channel_id=1, source_target_pairs={{64,0},{128,64},{192,128},{256,192},{320,256},{384,320},{448,384},... | collective-permute-start | bytes 786440 | tf_op jit(solution)/shard_map/while/body/eval_jaxpr/ppermute | solution.py:29
  419.8 7.8 %collective-permute-start.1 = (f32[64,1024]{1,0:T(8,128)S(1)}, f32[64,1024]{1,0:T(8,128)S(1)}, u32[]{:S(2)}, u32[]{:S(2)}) collective-permute-start(f32[64,1024]{1,0:T(8,128)S(1)} %convolution_add_fusion.5), channel_id=1, source_target_pairs={{64,0},{128,64},{192,128},{256,192},{320,256},{384,320},{448,384},... | collective-permute-start | bytes 786440 | tf_op jit(solution)/shard_map/while/body/eval_jaxpr/ppermute | solution.py:29
  428.0 8.2 %collective-permute-start.1 = (f32[64,1024]{1,0:T(8,128)S(1)}, f32[64,1024]{1,0:T(8,128)S(1)}, u32[]{:S(2)}, u32[]{:S(2)}) collective-permute-start(f32[64,1024]{1,0:T(8,128)S(1)} %convolution_add_fusion.5), channel_id=1, source_target_pairs={{64,0},{128,64},{192,128},{256,192},{320,256},{384,320},{448,384},... | collective-permute-start | bytes 786440 | tf_op jit(solution)/shard_map/while/body/eval_jaxpr/ppermute | solution.py:29
  (40 other events, 222.2 us)
Sparse Core Ops, SparseCore 0:
  335.5 173.6 all-gather.2
